TPU v7x, 128 devices: a whole 4x4x4 slice. The times are simulated.
128 devices in a mesh: seq: 8 (over y_hi, x), tensor: 16 (over y_lo, z, core).
Axes of the slice: x: 4, y: 4 (y_hi: 2, y_lo: 2; y = y_hi * 2 + y_lo), z: 4, core: 2. Of those that a mesh axis runs over, the one named last changes fastest.
Arguments:
- tokens: bfloat16 [4096, 4096], P('seq', 'tensor'), may hold values from -6 to 6
- seg_starts: int32 [8], replicated, may hold values from 0 to 4095, as said below
- gain_hyena: float32 [4096], replicated, may hold values from 0.1 to 1.9
- w_hyena_in: bfloat16 [4096, 3, 4096], P(None, None, 'tensor'), may hold values from -0.09375 to 0.09375
- hyena_filter: float32 [128, 4096], P(None, 'tensor'), may hold values from -1 to 1
- w_hyena_out: bfloat16 [4096, 4096], P('tensor'), may hold values from -0.125 to 0.125
- gain_attn: float32 [4096], replicated, may hold values from 0.1 to 1.9
- w_attn_in: bfloat16 [4096, 3, 4096], P(None, None, 'tensor'), may hold values from -0.75 to 0.75
- w_attn_out: bfloat16 [4096, 4096], P('tensor'), may hold values from -0.125 to 0.125
Outputs:
- block_out: float32 [4096, 4096], P('seq', 'tensor')
Inputs may be any that keep to these rules, and one draw needn't show every extreme that they name: Ascending and distinct, the first is 0, every other one at or after 4096 - 4096 // 4; genome i runs from seg_starts[i] to the next start, the last to the end of the window.
All inputs are finite; a program needn't handle non-finite values.
Results may differ from a plain program's by a relative error of at most 0.0079.
Values may be sent and summed in bfloat16 or wider, within the bound.
No kernel may reach another device: no remote copies, remote signals or barrier semaphores. Data moves between devices by JAX's collectives and lax.ppermute only.
A program may use at most 128 MiB of HBM per device.

v0:
```python
import jax
import jax.numpy as jnp
from jax import lax
from jax.sharding import PartitionSpec as P

HD = 128


def passed_along(block, axis, distance):
    devices = range(lax.axis_size(axis))
    route = [(i - distance, i) for i in devices if i - distance in devices]
    return lax.ppermute(block, axis, route)


def rms_scale(values, gain):
    factor = lax.rsqrt(jnp.mean(values * values, axis=-1, keepdims=True) + 1e-05)
    return (values * factor * gain).astype(jnp.bfloat16)


def segment_begin(positions, seg_starts):
    below = seg_starts[None, :] <= positions[:, None]
    return jnp.max(jnp.where(below, seg_starts[None, :], 0), axis=1)


def rotate(heads_in, positions):
    half_dim = heads_in.shape[-1] // 2
    freqs = 10000.0 ** (-2.0 * jnp.arange(half_dim, dtype=jnp.float32) / heads_in.shape[-1])
    angles = positions.astype(jnp.float32)[:, None] * freqs[None, :]
    cosine = jnp.cos(angles)[:, None, :]
    sine = jnp.sin(angles)[:, None, :]
    wide = heads_in.astype(jnp.float32)
    first = wide[..., :half_dim]
    second = wide[..., half_dim:]
    joined = jnp.concatenate(
        [first * cosine - second * sine, second * cosine + first * sine], axis=-1
    )
    return joined.astype(jnp.bfloat16)


def filter_conv(extended, taps, reach):
    length = taps.shape[0]
    out_rows = extended.shape[0] - (length - 1)
    group_size = 8

    def group_step(group, running):
        for inner in range(group_size):
            index = (group * group_size + inner).astype(jnp.int32)
            begin = length - 1 - index
            window_rows = lax.dynamic_slice_in_dim(extended, begin, out_rows, 0)
            keep = (index <= reach)[:, None]
            tap_row = lax.dynamic_index_in_dim(taps, index, 0, keepdims=True)
            running = running + jnp.where(keep, tap_row * window_rows, 0.0)
        return running

    start_value = jnp.zeros((out_rows, extended.shape[1]), jnp.float32)
    return lax.fori_loop(0, length // group_size, group_step, start_value)


def gather_rows(values):
    return lax.all_gather(values, "tensor", axis=1, tiled=True)


def attend(carry, key_piece, value_piece, queries, positions, begins):
    peak, total, running = carry
    key_pos = jnp.arange(key_piece.shape[0], dtype=jnp.int32)
    scores = jnp.einsum("qhd,khd->hqk", queries, key_piece, preferred_element_type=jnp.float32)
    scores = scores * queries.shape[-1] ** (-0.5)
    allowed = (key_pos[None, :] <= positions[:, None]) & (key_pos[None, :] >= begins[:, None])
    scores = jnp.where(allowed[None], scores, -jnp.inf)
    new_peak = jnp.max(scores, axis=2)
    safe_peak = jnp.where(jnp.isfinite(new_peak), new_peak, 0.0)
    weights = jnp.exp(scores - safe_peak[..., None])
    factor = jnp.exp(peak - safe_peak)
    total = total * factor + jnp.sum(weights, axis=2)
    update = jnp.einsum(
        "hqk,khd->hqd",
        weights.astype(jnp.bfloat16),
        value_piece,
        preferred_element_type=jnp.float32,
    )
    running = running * factor[..., None] + update
    return (new_peak, total, running)


def shards(
    tokens,
    seg_starts,
    gain_hyena,
    w_hyena_in,
    hyena_filter,
    w_hyena_out,
    gain_attn,
    w_attn_in,
    w_attn_out,
):
    row_count, local_width = tokens.shape
    full_width = w_hyena_in.shape[0]
    local_heads = local_width // HD
    taps_len = hyena_filter.shape[0]
    seq_index = lax.axis_index("seq")
    positions = seq_index * row_count + jnp.arange(row_count, dtype=jnp.int32)
    begins = segment_begin(positions, seg_starts)
    tokens_wide = tokens.astype(jnp.float32)
    whole = gather_rows(tokens_wide)
    normed = rms_scale(whole, gain_hyena)
    streams = jnp.dot(
        normed, w_hyena_in.reshape(full_width, 3 * local_width), preferred_element_type=jnp.float32
    )
    streams = streams.astype(jnp.bfloat16).reshape(row_count, 3, local_width)
    product = (streams[:, 1].astype(jnp.float32) * streams[:, 2].astype(jnp.float32)).astype(
        jnp.bfloat16
    )
    rim = passed_along(product[row_count - (taps_len - 1) :], "seq", 1)
    extended = jnp.concatenate([rim, product], axis=0).astype(jnp.float32)
    convolved = filter_conv(extended, hyena_filter, positions - begins)
    gated = (streams[:, 0].astype(jnp.float32) * convolved).astype(jnp.bfloat16)
    partial_hyena = jnp.dot(gated, w_hyena_out, preferred_element_type=jnp.float32)
    summed = lax.psum_scatter(partial_hyena, "tensor", scatter_dimension=1, tiled=True)
    middle = tokens_wide + summed
    middle_whole = gather_rows(middle)
    normed_attn = rms_scale(middle_whole, gain_attn)
    projected = jnp.dot(
        normed_attn,
        w_attn_in.reshape(full_width, 3 * local_width),
        preferred_element_type=jnp.float32,
    )
    projected = projected.astype(jnp.bfloat16).reshape(row_count, 3, local_heads, HD)
    queries = rotate(projected[:, 0], positions)
    rotated_keys = rotate(projected[:, 1], positions)
    local_values = projected[:, 2]
    start_carry = (
        jnp.full((local_heads, row_count), -jnp.inf, jnp.float32),
        jnp.zeros((local_heads, row_count), jnp.float32),
        jnp.zeros((local_heads, row_count, HD), jnp.float32),
    )
    final_carry = attend(
        start_carry,
        lax.all_gather(rotated_keys, "seq", axis=0, tiled=True),
        lax.all_gather(local_values, "seq", axis=0, tiled=True),
        queries,
        positions,
        begins,
    )
    context = final_carry[2] / final_carry[1][..., None]
    context = context.transpose(1, 0, 2).reshape(row_count, local_width).astype(jnp.bfloat16)
    partial_attn = jnp.dot(context, w_attn_out, preferred_element_type=jnp.float32)
    summed_attn = lax.psum_scatter(
        partial_attn.astype(jnp.bfloat16), "tensor", scatter_dimension=1, tiled=True
    ).astype(jnp.float32)
    return middle + summed_attn


def solution(mesh):
    placed = (
        P("seq", "tensor"),
        P(),
        P(),
        P(None, None, "tensor"),
        P(None, "tensor"),
        P("tensor", None),
        P(),
        P(None, None, "tensor"),
        P("tensor", None),
    )
    return jax.shard_map(
        shards, mesh=mesh, in_specs=placed, out_specs=P("seq", "tensor"), check_vma=False
    )
```

profile of v0, /device:TPU:22, one launch (start us, length us, event | category | flops | bytes accessed | tf_op | source)
XLA Modules:
  0.0 478.2 jit_solution(5104928755775515393)
XLA Ops:
  6.5 1.9 convert_element_type.78
  8.6 8.7 %copy.24 = bf16[4096,3,256]{0,2,1:T(8,128)(2,1)} copy(bf16[4096,3,256]{2,0,1:T(8,128)(2,1)} %param.14) | data formatting | bytes 12582912 | tf_op args[3]
  17.4 45.9 %all-gather.6.cloned.1.call-done = f32[512,4096]{1,0:T(8,128)} async-done(((f32[512,256]{1,0:T(8,128)}), f32[512,4096]{1,0:T(8,128)}) %all-gather.6.cloned.1.call-update) | async-done | bytes 8388624 | tf_op jit(solution)/shard_map/all_gather | solution.py:60
  63.4 4.2 multiply_reduce_fusion.1
  67.5 1.6 copy-done.4
  69.1 7.3 %fusion.22 = bf16[512,768]{1,0:T(8,128)(2,1)} fusion(bf16[4096,768]{0,1:T(8,128)(2,1)} %bitcast.79, f32[512,4096]{1,0:T(8,128)S(1)} %copy-done.4, f32[4096]{0:T(1024)S(1)} %copy-done.10, f32[512]{0:T(512)S(1)} %add_rsqrt_fusion.1), kind=kOutput, calls=%fused_computation.47 | convolution fusion | flops 3227910144 | bytes 15484928 | tf_op jit(solution)/shard_map/dot_general | solution.py:106
  76.4 2.4 copy.25
  79.9 1.3 collective-permute-start
  82.3 3.8 collective-permute-done
  87.1 1.3 copy.26
  88.4 38.7 %while.17 = (s32[]{:T(128)}, f32[512,256]{1,0:T(8,128)S(1)}, s32[512]{0:T(512)S(1)}, f32[128,256]{1,0:T(8,128)}, f32[639,256]{1,0:T(8,128)S(1)}, /*index=5*/s32[...) while((s32[]{:T(128)}, f32[512,256]{1,0:T(8,128)S(1)}, ...), condition=%wide.region_3.4_spmd.clone, body=%wide.region_2.3_spmd.clone.sunk | while | flops 3280963 | bytes 5278751 | solution.py:56
  89.6 1.3 fusion.69
  94.4 1.3 fusion.69
  99.3 1.3 fusion.69
  104.1 1.3 fusion.69
  127.4 5.5 %fusion.44 = f32[512,4096]{1,0:T(8,128)} fusion(bf16[256,4096]{1,0:T(8,128)(2,1)S(1)} %copy-done, f32[512,256]{0,1:T(8,128)S(1)} %copy.27, bf16[512,3,256]{0,2,1:T(8,128)(2,1)} %bitcast.83), kind=kOutput, calls=%fused_computation.63 | convolution fusion | flops 1074135040 | bytes 11272192 | tf_op jit(solution)/shard_map/dot_general | solution.py:117
  133.0 76.9 %reduce-scatter.3.cloned.1.call-done = f32[512,256]{1,0:T(8,128)} async-done(((f32[512,4096]{1,0:T(8,128)}), f32[512,256]{1,0:T(8,128)}) %reduce-scatter.3.cloned.1.call-update) | async-done | bytes 524304 | tf_op jit(solution)/shard_map/reduce_scatter | solution.py:118
  209.9 1.9 convert_add_fusion.1
  212.1 8.7 %copy.28 = bf16[4096,3,256]{0,2,1:T(8,128)(2,1)} copy(bf16[4096,3,256]{2,0,1:T(8,128)(2,1)} %param.18) | data formatting | bytes 12582912 | tf_op args[7]
  221.8 40.9 %all-gather.8.cloned.1.call-done = f32[512,4096]{1,0:T(8,128)} async-done(((f32[512,256]{1,0:T(8,128)}), f32[512,4096]{1,0:T(8,128)}) %all-gather.8.cloned.1.call-update) | async-done | bytes 8388624 | tf_op jit(solution)/shard_map/all_gather | solution.py:60
  262.7 4.2 multiply_reduce_fusion
  266.9 1.6 copy-done.5
  268.5 6.4 %fusion.21 = bf16[512,768]{1,0:T(8,128)(2,1)S(1)} fusion(bf16[4096,768]{0,1:T(8,128)(2,1)} %bitcast.80, f32[512,4096]{1,0:T(8,128)S(1)} %copy-done.5, f32[4096]{0:T(1024)S(1)} %copy-done.11, f32[512]{0:T(512)S(1)} %add_rsqrt_fusion), kind=kOutput, calls=%fused_computation.46 | convolution fusion | flops 3227910144 | bytes 15484928 | tf_op jit(solution)/shard_map/dot_general | solution.py:122
  278.2 2.4 fusion.12
  280.6 49.6 %all-gather.10.cloned.1.call-done = bf16[4096,2,128]{2,0,1:T(8,128)(2,1)} async-done(((bf16[512,2,128]{2,0,1:T(8,128)(2,1)}), bf16[4096,2,128]{2,0,1:T(8,128)(2,1)}) %all-gather.10.cloned.1.call-update) | async-done | bytes 2097168 | tf_op jit(solution)/shard_map/all_gather | solution.py:138
  330.2 5.3 %fusion.7 = (f32[2,512]{1,0:T(2,128)S(1)}, f32[2,512,4096]{2,1,0:T(8,128)S(1)}) fusion(pred[512,4096]{1,0:T(8,128)(4,1)S(1)} %fusion.12, bf16[4096,2,128]{2,0,1:T(8,128)(2,1)} %all-gather.10.cloned.1.call-done, bf16[512,2,64]{2,0,1:T(8,128)(2,1)S(1)} %get-tuple-element.236, bf16[512,2,64]{2,0,1:T(8,128)(2,1)S(1)} %get-tuple-element.235), kind=kOutput, calls=%fused_computation.26 | convolution fusion | flops 1086848000 | bytes 21237760 | tf_op jit(solution)/shard_map/qhd,khd->hqk/dot_general | solution.py:66
  335.6 4.6 fusion.8
  341.3 47.3 %all-gather.12.cloned.1.call-done = bf16[4096,1,2,128]{0,3,2,1:T(8,128)(2,1)} async-done(((bf16[512,1,2,128]{0,3,2,1:T(8,128)(2,1)}), bf16[4096,1,2,128]{0,3,2,1:T(8,128)(2,1)}) %all-gather.12.cloned.1.call-update) | async-done | bytes 2097168 | tf_op jit(solution)/shard_map/all_gather | solution.py:139
  388.6 9.1 %fusion.38 = bf16[512,2,128]{0,2,1:T(8,128)(2,1)S(1)} fusion(bf16[4096,1,2,128]{0,3,2,1:T(8,128)(2,1)} %all-gather.12.cloned.1.call-done, f32[2,512,4096]{2,1,0:T(8,128)} %copy-done.2, f32[2,512]{1,0:T(2,128)S(1)} %is-finite_select_fusion, pred[512,4096]{1,0:T(8,128)(4,1)} %copy-done.3, f32[512,2]{0,1:T(2,128)S(1)} %get-tuple-element.245, ...), kind=kOutput, calls=%fused_computation.51 | convolution fusion | flops 1090912256 | bytes 21245952 | tf_op jit(solution)/shard_map/hqk,khd->hqd/dot_general | solution.py:75
  397.7 3.2 convolution_convert_fusion
  401.0 68.6 %reduce-scatter.5.cloned.1.call-done = bf16[512,256]{1,0:T(8,128)(2,1)} async-done(((bf16[512,4096]{1,0:T(8,128)(2,1)}), bf16[512,256]{1,0:T(8,128)(2,1)}) %reduce-scatter.5.cloned.1.call-update) | async-done | bytes 262160 | tf_op jit(solution)/shard_map/reduce_scatter | solution.py:147
  469.5 1.8 convert_add_fusion
  (100 shorter events, 40.7 us)
Async XLA Ops:
  6.5 120.8 %copy-start = (bf16[256,4096]{1,0:T(8,128)(2,1)S(1)}, bf16[256,4096]{1,0:T(8,128)(2,1)}, u32[]{:S(2)}) copy-start(bf16[256,4096]{1,0:T(8,128)(2,1)} %param.16) | copy-start | bytes 6291460
  6.5 10.8 %copy-start.9 = (s32[8]{0:T(128)S(1)}, s32[8]{0:T(128)}, u32[]{:S(2)}) copy-start(s32[8]{0:T(128)} %param.12) | copy-start | bytes 100
  6.5 56.8 %all-gather.6.cloned.1.call-start = ((), (), s32[]{:S(2)}) async-start(), calls=%async_computation.2 | async-start | bytes 8912896 | tf_op jit(solution)/shard_map/all_gather | solution.py:60
  8.5 201.4 %reduce-scatter.3.cloned.1.call-start = ((), (), s32[]{:S(2)}) async-start(), calls=%async_computation.3 | async-start | bytes 8912896 | tf_op jit(solution)/shard_map/reduce_scatter | solution.py:118
  8.6 59.0 %copy-start.10 = (f32[4096]{0:T(1024)S(1)}, f32[4096]{0:T(1024)}, u32[]{:S(2)}) copy-start(f32[4096]{0:T(1024)} %param.13) | copy-start | bytes 49156
  63.4 5.8 %copy-start.4 = (f32[512,4096]{1,0:T(8,128)S(1)}, f32[512,4096]{1,0:T(8,128)}, u32[]{:S(2)}) copy-start(f32[512,4096]{1,0:T(8,128)} %all-gather.6.cloned.1.call-done) | copy-start | bytes 25165828
  79.9 6.2 %collective-permute-start = (bf16[127,256]{0,1:T(8,128)(2,1)S(1)}, bf16[127,256]{0,1:T(8,128)(2,1)S(1)}, u32[]{:S(2)}, u32[]{:S(2)}) collective-permute-start(bf16[127,256]{0,1:T(8,128)(2,1)S(1)} %slice_bitcast_fusion.2), channel_id=1, source_target_pairs={{0,16},{16,32},{32,48},{48,64},{64,80},{80,96},{96,112},{1,17},{17... | collective-permute-start | bytes 195080 | tf_op jit(solution)/shard_map/ppermute | solution.py:12
  127.4 82.5 %copy-start.8 = (bf16[512,256]{1,0:T(8,128)(2,1)S(1)}, bf16[512,256]{1,0:T(8,128)(2,1)}, u32[]{:S(2)}) copy-start(bf16[512,256]{1,0:T(8,128)(2,1)} %param.11) | copy-start | bytes 786436
  132.9 129.8 %all-gather.8.cloned.1.call-start = ((), (), s32[]{:S(2)}) async-start(), calls=%async_computation.4 | async-start | bytes 8912896 | tf_op jit(solution)/shard_map/all_gather | solution.py:60
  211.8 55.1 %copy-start.11 = (f32[4096]{0:T(1024)S(1)}, f32[4096]{0:T(1024)}, u32[]{:S(2)}) copy-start(f32[4096]{0:T(1024)} %param.17) | copy-start | bytes 49156
  211.8 118.4 %all-gather.10.cloned.1.call-start = ((), (), s32[]{:S(2)}) async-start(), calls=%async_computation.5 | async-start | bytes 2359296 | tf_op jit(solution)/shard_map/all_gather | solution.py:138
  262.7 5.8 %copy-start.5 = (f32[512,4096]{1,0:T(8,128)S(1)}, f32[512,4096]{1,0:T(8,128)}, u32[]{:S(2)}) copy-start(f32[512,4096]{1,0:T(8,128)} %all-gather.8.cloned.1.call-done) | copy-start | bytes 25165828
  277.0 111.6 %all-gather.12.cloned.1.call-start = ((), (), s32[]{:S(2)}) async-start(), calls=%async_computation.7 | async-start | bytes 2359296 | tf_op jit(solution)/shard_map/all_gather | solution.py:139
  277.9 191.6 %reduce-scatter.5.cloned.1.call-start = ((), (), s32[]{:S(2)}) async-start(), calls=%async_computation.6 | async-start | bytes 4456448 | tf_op jit(solution)/shard_map/reduce_scatter | solution.py:147
  280.6 54.9 %copy-start.3 = (pred[512,4096]{1,0:T(8,128)(4,1)}, pred[512,4096]{1,0:T(8,128)(4,1)S(1)}, u32[]{:S(2)}) copy-start(pred[512,4096]{1,0:T(8,128)(4,1)S(1)} %fusion.12) | copy-start | bytes 6291460
  335.5 5.7 %copy-start.2 = (f32[2,512,4096]{2,1,0:T(8,128)}, f32[2,512,4096]{2,1,0:T(8,128)S(1)}, u32[]{:S(2)}) copy-start(f32[2,512,4096]{2,1,0:T(8,128)S(1)} %get-tuple-element.249) | copy-start | bytes 50331652
  388.6 9.1 %copy-start.7 = (bf16[256,4096]{1,0:T(8,128)(2,1)S(1)}, bf16[256,4096]{1,0:T(8,128)(2,1)}, u32[]{:S(2)}) copy-start(bf16[256,4096]{1,0:T(8,128)(2,1)} %param.19) | copy-start | bytes 6291460
  388.6 82.8 %copy-start.1 = (bf16[256,4096]{1,0:T(8,128)(2,1)S(1)}, bf16[256,4096]{1,0:T(8,128)(2,1)}, u32[]{:S(2)}) copy-start(bf16[256,4096]{1,0:T(8,128)(2,1)} %param.16) | copy-start | bytes 6291460
  397.7 71.8 %copy-start.6 = (f32[512,256]{1,0:T(8,128)S(1)}, f32[512,256]{1,0:T(8,128)}, u32[]{:S(2)}) copy-start(f32[512,256]{1,0:T(8,128)} %convert_add_fusion.1) | copy-start | bytes 1572868
Sparse Core Ops, SparseCore 0:
  9.0 54.2 all-gather.5
  133.1 76.7 reduce-scatter.2
  211.9 50.7 all-gather.7
  277.1 53.0 all-gather.9
  332.2 56.3 all-gather.11
  401.1 68.3 reduce-scatter.4
where the time goes:
time: 480 us; the launch traced here: 478 us
  waiting for transfers between devices  333 us (69%)
  other arithmetic  46.7 us (10%)
  local copies, waits for them, and re-layouts  43.6 us (9%)
  matrix products  36.8 us (8%)
  between operations  13.7 us (3%)
    all_gather x2, waiting for transfers between devices, gather_rows(): return lax.all_gather(values, 'tensor', axis=1, tiled=True)  86.8 us
    reduce_scatter x1, waiting for transfers between devices, shards(): lax.psum_scatter(partial_hyena, 'tensor', scatter_dimension=1, tiled=True)  76.9 us
    reduce_scatter x1, waiting for transfers between devices, shards(): lax.psum_scatter(partial_attn.astype(jnp.bfloat16), 'tensor', scatter_dim...  68.6 us
    all_gather x1, waiting for transfers between devices, shards(): lax.all_gather(rotated_keys, 'seq', axis=0, tiled=True)  49.6 us
    all_gather x1, waiting for transfers between devices, shards(): lax.all_gather(local_values, 'seq', axis=0, tiled=True)  47.3 us
    unnamed x28, local copies, waits for them, and re-layouts  24 us
    add x16, other arithmetic, group_step(): running = running + jnp.where(keep, tap_row * window_rows, 0.0)  19.9 us
    dynamic_slice x16, local copies, waits for them, and re-layouts, group_step(): tap_row = lax.dynamic_index_in_dim(taps, index, 0, keepdims=True)  16.3 us
  transfers between devices with their start and end apart: 7, of which 7 were waited for; matrix products, arithmetic and copies ran while one was open for 7% of the time, Pallas kernels for 0%

commit v1 on v0

v1 whole, which is shorter than its diff:
```python
import functools
import math

import jax
import jax.numpy as jnp
from jax import lax
from jax.experimental import pallas as pl
from jax.experimental.pallas import tpu as pltpu
from jax.sharding import PartitionSpec as P

HD = 128
TAPS = 128
BF = jnp.bfloat16
F32 = jnp.float32
NEG = -1e30
VMEM = pl.BlockSpec(memory_space=pltpu.VMEM)
SMEM = pl.BlockSpec(memory_space=pltpu.SMEM)
LIMIT = 40 * 2**20


def tensor_route(move):
    pairs = []
    for t in range(16):
        y, z, c = move(t // 8, t // 2 % 4, t % 2)
        pairs.append((t, (y % 2) * 8 + (z % 4) * 2 + c % 2))
    return pairs


ROUTE_Y = tensor_route(lambda y, z, c: (y + 1, z, c))
ROUTE_UP = tensor_route(lambda y, z, c: (y, z + 1, c))
ROUTE_DOWN = tensor_route(lambda y, z, c: (y, z - 1, c))
ROUTE_FAR = tensor_route(lambda y, z, c: (y, z + 2, c))
ROUTE_CORE = tensor_route(lambda y, z, c: (y, z, c + 1))


def send(block, route, axis="tensor"):
    return lax.ppermute(block, axis, route)


def gather_tensor(block):
    side = send(block, ROUTE_Y)
    below = send(block, ROUTE_UP)
    above = send(block, ROUTE_DOWN)
    far = send(block, ROUTE_FAR)
    side_below = send(side, ROUTE_UP)
    side_above = send(side, ROUTE_DOWN)
    side_far = send(far, ROUTE_Y)
    mine = [block, above, far, below, side, side_above, side_far, side_below]
    return mine + [send(one, ROUTE_CORE) for one in mine]


EARLY = [0, 8, 4, 12, 1, 9, 3, 11]
LATE = [2, 10, 5, 13, 7, 15, 6, 14]


def relative_order(position):
    y, z, c = position // 8, position // 2 % 4, position % 2
    out = []
    for dc in range(2):
        for dy in range(2):
            for dz in range(4):
                out.append(((y + dy) % 2) * 8 + ((z + dz) % 4) * 2 + (c + dc) % 2)
    return jnp.stack(out).astype(jnp.int32)


def scatter_tensor(mine, other):
    received = send(other, ROUTE_CORE)

    def part(i):
        return (mine[i].astype(F32) + received[i].astype(F32)).astype(BF)

    side = send(part(6), ROUTE_Y)
    up = send(jnp.stack([part(1), part(5)]), ROUTE_UP)
    down = send(jnp.stack([part(3), part(7)]), ROUTE_DOWN)
    two = (mine[2].astype(F32) + received[2].astype(F32) + side.astype(F32)).astype(BF)
    far = send(two, ROUTE_FAR)
    across = mine[4].astype(F32) + received[4].astype(F32) + up[1].astype(F32) + down[1].astype(F32)
    back = send(across.astype(BF), ROUTE_Y)
    near = mine[0].astype(F32) + received[0].astype(F32) + up[0].astype(F32) + down[0].astype(F32)
    return near + far.astype(F32) + back.astype(F32)


def project_kernel(epilogue, count, carried, order, *refs):
    refs = list(refs)
    blocks = [refs.pop(0) for _ in range(count)]
    gain = refs.pop(0)
    weight = refs.pop(0)
    sums_in, square_in = (refs.pop(0), refs.pop(0)) if carried else (None, None)
    tables = (refs.pop(0), refs.pop(0)) if epilogue == "rotate" or epilogue == "keys" else None
    scaled = refs.pop()
    square = refs.pop()
    outs = refs
    step = pl.program_id(0)

    @pl.when(step == 0)
    def _():
        total = None
        for k in range(count):
            wide = blocks[k][...].astype(F32)
            scaled[k] = (wide * gain[order[k]]).astype(BF)
            part = wide * wide
            total = part if total is None else total + part
        total = jnp.sum(total, axis=1, keepdims=True)
        if carried:
            total = total + square_in[...]
        square[...] = total

    acc = sums_in[0] if carried else None
    for k in range(count):
        term = jnp.dot(scaled[k], weight[0, order[k]], preferred_element_type=F32)
        acc = term if acc is None else acc + term
    if epilogue == "sums":
        outs[0][0] = acc
        outs[1][...] = square[...]
        return
    width = 16 * acc.shape[1]
    acc = acc * lax.rsqrt(square[...] / width + 1e-05)
    half = acc.astype(BF)

    def rotated():
        cosine, sine = tables
        parts = []
        for h in range(half.shape[1] // HD):
            head = half[:, h * HD : (h + 1) * HD].astype(F32)
            turned = pltpu.roll(head, HD // 2, 1)
            parts.append((head * cosine[...] + turned * sine[...]).astype(BF))
        return jnp.concatenate(parts, axis=1)

    if epilogue == "plain":
        outs[0][...] = half
    elif epilogue == "rotate":
        outs[0][...] = rotated()
    elif epilogue == "product":

        @pl.when(step == 0)
        def _():
            outs[0][...] = half

        @pl.when(step == 1)
        def _():
            outs[0][...] = (outs[0][...].astype(F32) * half.astype(F32)).astype(BF)

    else:
        width = half.shape[1]

        @pl.when(step == 0)
        def _():
            outs[0][:, 0:width] = rotated()

        @pl.when(step == 1)
        def _():
            outs[0][:, width : 2 * width] = half


def project(epilogue, blocks, order, gain, weight, first, steps, carry=None, tables=None):
    rows, wide = blocks[0].shape
    cols = weight.shape[3]
    count = len(blocks)

    def whole(shape):
        return pl.BlockSpec(shape, lambda i, o: (0,) * len(shape))

    in_specs = [whole((rows, wide))] * count + [whole(gain.shape)]
    in_specs.append(pl.BlockSpec((1, 16, wide, cols), lambda i, o: (first + i, 0, 0, 0)))
    operands = [*blocks, gain, weight]
    if carry is not None:
        in_specs += [pl.BlockSpec((1, rows, cols), lambda i, o: (first + i, 0, 0)), whole((rows, 1))]
        operands += list(carry)
    if tables is not None:
        in_specs += [whole(tables[0].shape)] * 2
        operands += list(tables)
    if epilogue == "sums":
        out_shape = (jax.ShapeDtypeStruct((steps, rows, cols), F32), jax.ShapeDtypeStruct((rows, 1), F32))
        out_specs = (pl.BlockSpec((1, rows, cols), lambda i, o: (i, 0, 0)), whole((rows, 1)))
    else:
        out_cols = 2 * cols if epilogue == "keys" else cols
        out_shape = jax.ShapeDtypeStruct((rows, out_cols), BF)
        out_specs = whole((rows, out_cols))
    return pl.pallas_call(
        functools.partial(project_kernel, epilogue, count, carry is not None),
        out_shape=out_shape,
        grid_spec=pltpu.PrefetchScalarGridSpec(
            num_scalar_prefetch=1,
            grid=(steps,),
            in_specs=in_specs,
            out_specs=out_specs,
            scratch_shapes=[pltpu.VMEM((rows, 1), F32), pltpu.VMEM((count, rows, wide), BF)],
        ),
        compiler_params=pltpu.CompilerParams(vmem_limit_bytes=LIMIT),
        cost_estimate=pl.CostEstimate(
            flops=2 * rows * wide * count * cols * steps,
            bytes_accessed=2 * (rows * wide * count + wide * 16 * cols * steps + 2 * rows * cols),
            transcendentals=0,
        ),
        name=f"project_{epilogue}",
    )(order, *operands)


def spread_kernel(order, x, weight, out):
    wide = out.shape[2]
    for k in range(out.shape[0]):
        columns = pl.ds(pl.multiple_of(order[k] * wide, wide), wide)
        out[k] = jnp.dot(x[...], weight[:, columns], preferred_element_type=F32).astype(BF)


def spread(x, weight, order):
    rows, wide = x.shape
    count = order.shape[0]
    return pl.pallas_call(
        spread_kernel,
        out_shape=jax.ShapeDtypeStruct((count, rows, wide), BF),
        in_specs=[SMEM, VMEM, VMEM],
        out_specs=VMEM,
        compiler_params=pltpu.CompilerParams(vmem_limit_bytes=LIMIT),
        cost_estimate=pl.CostEstimate(
            flops=2 * rows * wide * wide * count,
            bytes_accessed=2 * (rows * wide + wide * wide * count + rows * wide * count),
            transcendentals=0,
        ),
        name="spread",
    )(order, x, weight)


def filter_kernel(tile, extended, taps, reach, gate, out, shifted):
    total = extended.shape[0]
    rows = out.shape[0]
    wide = extended[...].astype(F32)
    shifted[0] = wide
    for r in range(1, 8):
        shifted[r, 8:total] = shifted[0, 8 - r : total - r]

    def row_tile(i, carry):
        base = pl.multiple_of(i * tile, tile)
        limit = jnp.broadcast_to(reach[pl.ds(base, tile), :], (tile, HD))
        parts = out.shape[1] // HD

        def group(a, accs):
            start = pl.multiple_of(base + TAPS - 8 * a, 8)
            tap_rows = taps[pl.ds(pl.multiple_of(8 * a, 8), 8), :]
            accs = list(accs)
            for r in range(8):
                keep = limit >= 8 * a + r
                for p in range(parts):
                    lanes = slice(p * HD, (p + 1) * HD)
                    window = shifted[r, pl.ds(start, tile), lanes]
                    term = tap_rows[r : r + 1, lanes] * window
                    accs[p] = accs[p] + jnp.where(keep, term, 0.0)
            return tuple(accs)

        zero = tuple(jnp.zeros((tile, HD), F32) for _ in range(parts))
        accs = lax.fori_loop(0, TAPS // 8, group, zero)
        for p in range(parts):
            lanes = slice(p * HD, (p + 1) * HD)
            query = gate[pl.ds(base, tile), lanes].astype(F32)
            out[pl.ds(base, tile), lanes] = (query * accs[p]).astype(BF)
        return carry

    lax.fori_loop(0, rows // tile, row_tile, 0)


def filtered(extended, taps, reach, gate):
    rows, width = gate.shape
    return pl.pallas_call(
        functools.partial(filter_kernel, 64),
        out_shape=jax.ShapeDtypeStruct((rows, width), BF),
        in_specs=[VMEM] * 4,
        out_specs=VMEM,
        scratch_shapes=[pltpu.VMEM((8, rows + TAPS, width), F32)],
        compiler_params=pltpu.CompilerParams(vmem_limit_bytes=LIMIT),
        cost_estimate=pl.CostEstimate(
            flops=6 * TAPS * rows * width * 40, bytes_accessed=8 * rows * width, transcendentals=0
        ),
        name="filtered",
    )(extended, taps, reach, gate)


def attend_kernel(last, width, me_ref, q_ref, begin_ref, *refs):
    refs = list(refs)
    pieces = [refs.pop(0) for _ in range(4)]
    if last:
        before = [refs.pop(0) for _ in range(3)]
        (out,) = refs[:1]
        peak, total, running = refs[1:]
    else:
        peak, total, running = refs
    me = me_ref[0]
    rows = q_ref.shape[0]
    heads = width // HD
    chunk = 128
    scale = HD**-0.5 * math.log2(math.e)
    x = me % 4
    row_block = me // 4
    if last:
        peak[...] = before[0][...]
        total[...] = before[1][...]
        running[...] = before[2][...]
    else:
        peak[...] = jnp.full(peak.shape, NEG, F32)
        total[...] = jnp.zeros(total.shape, F32)
        running[...] = jnp.zeros(running.shape, F32)
    for i, dx in enumerate((0, 3, 1, 2)):
        owner = (row_block - 1 if last else row_block) * 4 + (x + dx) % 4

        @pl.when((row_block > 0) if last else (owner <= me))
        def _(i=i, owner=owner):
            piece = pieces[i]

            def one(step, carry):
                base = pl.multiple_of(step * chunk, chunk)
                span = pl.ds(base, chunk)
                begin = begin_ref[span, :]
                if last:
                    open_row = begin <= owner * rows
                else:
                    key_at = owner * rows + lax.broadcasted_iota(jnp.int32, (chunk, rows), 1)
                    row_at = me * rows + base + lax.broadcasted_iota(jnp.int32, (chunk, rows), 0)
                    allowed = (key_at <= row_at) & (key_at >= begin)
                for h in range(heads):
                    lanes = slice(h * HD, (h + 1) * HD)
                    keys = piece[:, lanes]
                    values = piece[:, width + h * HD : width + (h + 1) * HD]
                    scores = lax.dot_general(
                        q_ref[span, lanes], keys, (((1,), (1,)), ((), ())), preferred_element_type=F32
                    )
                    old = peak[h, span, :]
                    if last:
                        top = jnp.max(scores, axis=1, keepdims=True)
                        new = jnp.where(open_row, jnp.maximum(old, top), old)
                        level = jnp.where(open_row, new, -NEG)
                    else:
                        scores = jnp.where(allowed, scores, NEG)
                        new = jnp.maximum(old, jnp.max(scores, axis=1, keepdims=True))
                        level = new
                    weights = jnp.exp2((scores - level) * scale)
                    factor = jnp.exp2((old - new) * scale)
                    peak[h, span, :] = new
                    total[h, span, :] = total[h, span, :] * factor + jnp.sum(weights, axis=1, keepdims=True)
                    update = jnp.dot(weights.astype(BF), values, preferred_element_type=F32)
                    running[h, span, :] = running[h, span, :] * factor + update
                return carry

            lax.fori_loop(0, rows // chunk, one, 0)

    if last:
        for h in range(heads):
            out[:, h * HD : (h + 1) * HD] = (running[h] / total[h]).astype(BF)


def attend(me, queries, begins, pieces, before=None):
    rows, width = queries.shape
    heads = width // HD
    state = [(heads, rows, 1), (heads, rows, 1), (heads, rows, HD)]
    last = before is not None
    if last:
        out_shape = jax.ShapeDtypeStruct((rows, width), BF)
        scratch = [pltpu.VMEM(s, F32) for s in state]
        out_specs = VMEM
    else:
        out_shape = tuple(jax.ShapeDtypeStruct(s, F32) for s in state)
        scratch = []
        out_specs = (VMEM,) * 3
    before = tuple(before) if last else ()
    return pl.pallas_call(
        functools.partial(attend_kernel, last, width),
        out_shape=out_shape,
        in_specs=[SMEM] + [VMEM] * (2 + 4 + len(before)),
        out_specs=out_specs,
        scratch_shapes=scratch,
        compiler_params=pltpu.CompilerParams(vmem_limit_bytes=LIMIT),
        cost_estimate=pl.CostEstimate(
            flops=4 * rows * rows * width * 4 * 3, bytes_accessed=2 * 10 * rows * width, transcendentals=rows * rows * 8
        ),
        name="attend_far" if last else "attend_near",
    )(me, queries, begins, *pieces, *before)


def row_ring(piece, lines):
    full = lines == (1,)

    def route(pairs):
        return [(y * 4 + a, y * 4 + b) for y in lines for a, b in pairs]

    up = [(0, 1), (1, 2), (2, 3)] + ([(3, 0)] if full else [])
    down = [(0, 3), (1, 0)] + ([(2, 1), (3, 2)] if full else [])
    up_half = [(1, 2), (2, 3)] + ([(3, 0), (0, 1)] if full else [])
    down_half = [(3, 2), (0, 3)] + ([(1, 0), (2, 1)] if full else [])
    half = piece.shape[0] // 2
    left = send(piece, route(up), "seq")
    right = send(piece, route(down), "seq")
    far = jnp.concatenate(
        [send(left[:half], route(up_half), "seq"), send(right[half:], route(down_half), "seq")], axis=0
    )
    return [piece, left, right, far]


def segment_begin(positions, seg_starts):
    below = seg_starts[None, :] <= positions[:, None]
    return jnp.max(jnp.where(below, seg_starts[None, :], 0), axis=1)


def rotation_tables(positions):
    half_dim = HD // 2
    freqs = 10000.0 ** (-2.0 * jnp.arange(half_dim, dtype=F32) / HD)
    angles = positions.astype(F32)[:, None] * freqs[None, :]
    cosine = jnp.cos(angles)
    sine = jnp.sin(angles)
    return jnp.concatenate([cosine, cosine], axis=1), jnp.concatenate([-sine, sine], axis=1)


def shards(
    tokens,
    seg_starts,
    gain_hyena,
    w_hyena_in,
    hyena_filter,
    w_hyena_out,
    gain_attn,
    w_attn_in,
    w_attn_out,
):
    rows, width = tokens.shape
    me = lax.axis_index("seq").astype(jnp.int32)
    order = relative_order(lax.axis_index("tensor"))
    early = order[jnp.array(EARLY)]
    late = order[jnp.array(LATE)]
    positions = me * rows + jnp.arange(rows, dtype=jnp.int32)
    begins = segment_begin(positions, seg_starts)
    reach = (positions - begins)[:, None]
    begins = begins[:, None]
    tables = rotation_tables(positions)

    def streams_of(block, gain, weight, kinds, tables=None):
        blocks = gather_tensor(block)
        gain = gain.reshape(16, 1, width)
        weight = weight.reshape(16, width, 3, width).transpose(2, 0, 1, 3)
        carry = project("sums", [blocks[i] for i in EARLY], early, gain, weight, 0, 3)
        rest = [blocks[i] for i in LATE]
        back = project(kinds[0], rest, late, gain, weight, 1, 2, carry, tables)
        front = project(kinds[1], rest, late, gain, weight, 0, 1, carry, tables)
        return front, back

    def summed_over_tensor(values, weight):
        other = spread(values, weight, order[8:])
        return scatter_tensor(spread(values, weight, order[:8]), other)

    gate, product = streams_of(tokens, gain_hyena, w_hyena_in, ("product", "plain"))
    rim = send(product[rows - TAPS :], [(i, i + 1) for i in range(7)], "seq")
    tail = filtered(product, hyena_filter, reach[TAPS:], gate[TAPS:])
    head = filtered(
        jnp.concatenate([rim, product[:TAPS]], axis=0), hyena_filter, reach[:TAPS], gate[:TAPS]
    )
    gated = jnp.concatenate([head, tail], axis=0)
    middle = tokens.astype(F32) + summed_over_tensor(gated, w_hyena_out)
    queries, own = streams_of(middle.astype(BF), gain_attn, w_attn_in, ("keys", "rotate"), tables)
    below = send(own, [(x, 4 + x) for x in range(4)], "seq")
    near = row_ring(own, (0, 1))
    far = row_ring(below, (1,))
    where = me[None]
    state = attend(where, queries, begins, near)
    context = attend(where, queries, begins, far, state)
    return middle + summed_over_tensor(context, w_attn_out)


def solution(mesh):
    placed = (
        P("seq", "tensor"),
        P(),
        P(),
        P(None, None, "tensor"),
        P(None, "tensor"),
        P("tensor", None),
        P(),
        P(None, None, "tensor"),
        P("tensor", None),
    )
    return jax.shard_map(
        shards, mesh=mesh, in_specs=placed, out_specs=P("seq", "tensor"), check_vma=False
    )
```

time: 480 us -> 255 us (0.53)
  waiting for transfers between devices: 333 us -> 105 us
  Pallas kernels: 0 us -> 60.9 us
  starting transfers between devices: 1.9 us -> 54.8 us
  matrix products: 36.8 us -> 0 us
  other arithmetic: 46.7 us -> 12.2 us
  local copies, waits for them, and re-layouts: 43.6 us -> 20.5 us
  between operations: 13.7 us -> 0.82 us
    all_gather x4 -> x0, waiting for transfers between devices: 184 us -> none  [the longest x2 86.8 us: gather_rows(): return lax.all_gather(values, 'tensor', axis=1, tiled=True)]
    reduce_scatter x2 -> x0, waiting for transfers between devices: 145 us -> none  [the longest x1 76.9 us: shards(): lax.psum_scatter(partial_hyena, 'tensor', scatter_dimension=1, tiled=True)]
    ppermute x1 -> x52, waiting for transfers between devices: 3.76 us -> 105 us  [send(): return lax.ppermute(block, axis, route)]
    pallas_call x0 -> x14, Pallas kernels: none -> 60.9 us  [the longest x2 27.8 us: attend(): pl.pallas_call(functools.partial(attend_kernel, last, width), out_shape=o...]
    ppermute x1 -> x52, starting transfers between devices: 1.29 us -> 54.8 us  [send(): return lax.ppermute(block, axis, route)]
    dot_general x6 -> x0, matrix products: 36.8 us -> none  [the longest x1 9.11 us: attend(): jnp.einsum('hqk,khd->hqd', weights.astype(jnp.bfloat16), value_piece, pre...]
    add x19 -> x2, other arithmetic: 23.5 us -> 1.02 us  [the longest x1 1.02 us: shards(): return middle + summed_over_tensor(context, w_attn_out)]
    dynamic_slice x16 -> x0, local copies, waits for them, and re-layouts: 16.3 us -> none  [group_step(): tap_row = lax.dynamic_index_in_dim(taps, index, 0, keepdims=True)]
  transfers between devices with their start and end apart: 7 -> 52, of which waited for: 7 -> 25; matrix products, arithmetic and copies ran while one was open for 7% -> 5% of each run, Pallas kernels for 0% -> 13%
where the time goes in v1:
time: 255 us
  waiting for transfers between devices  105 us (41%)
  Pallas kernels  60.9 us (24%)
  starting transfers between devices  54.8 us (21%)
  local copies, waits for them, and re-layouts  20.5 us (8%)
  other arithmetic  12.2 us (5%)
    ppermute x52, waiting for transfers between devices, send(): return lax.ppermute(block, axis, route)  105 us
    ppermute x52, starting transfers between devices, send(): return lax.ppermute(block, axis, route)  54.8 us
    pallas_call x2, Pallas kernels, attend(): pl.pallas_call(functools.partial(attend_kernel, last, width), out_shape=o...  27.8 us
    pallas_call x6, Pallas kernels, project(): pl.pallas_call(functools.partial(project_kernel, epilogue, count, carry i...  16.9 us
    unnamed x62, local copies, waits for them, and re-layouts  13.6 us
    pallas_call x2, Pallas kernels, filtered(): pl.pallas_call(functools.partial(filter_kernel, 64), out_shape=jax.ShapeD...  9.75 us
    pallas_call x4, Pallas kernels, spread(): pl.pallas_call(spread_kernel, out_shape=jax.ShapeDtypeStruct((count, rows...  6.37 us
  transfers between devices with their start and end apart: 52, of which 25 were waited for; matrix products, arithmetic and copies ran while one was open for 5% of the time, Pallas kernels for 13%

profile of v1, /device:TPU:22, one launch (start us, length us, event | category | flops | bytes accessed | tf_op | source)
XLA Modules:
  0.0 254.5 jit_solution(15055679979699443171)
XLA Ops:
  1.3 3.9 %collective-permute-start = (bf16[512,256]{1,0:T(8,128)(2,1)}, bf16[512,256]{1,0:T(8,128)(2,1)S(1)}, u32[]{:S(2)}, u32[]{:S(2)}) collective-permute-start(bf16[512,256]{1,0:T(8,128)(2,1)} %refs_0_.1), channel_id=1, source_target_pairs={{0,4},{1,5},{2,6},{3,7},{4,0},{5,1},{6,2},{7,3},{8,12},{9,13},{10,... | collective-permute-start | bytes 786440 | tf_op jit(solution)/shard_map/ppermute | solution.py:37
  8.3 4.0 %collective-permute-start.3 = (bf16[512,256]{1,0:T(8,128)(2,1)S(1)}, bf16[512,256]{1,0:T(8,128)(2,1)S(1)}, u32[]{:S(2)}, u32[]{:S(2)}) collective-permute-start(bf16[512,256]{1,0:T(8,128)(2,1)S(1)} %collective-permute-done.2.refs_2_), channel_id=1, source_target_pairs={{0,6},{1,7},{2,0},{3,1},{4,2},{5,3},{6,4},{7,5},{8,14},{9,15},{10,... | collective-permute-start | bytes 786440 | tf_op jit(solution)/shard_map/ppermute | solution.py:37
  14.2 5.1 %collective-permute-done.11.refs_4_ = bf16[512,256]{1,0:T(8,128)(2,1)S(1)} collective-permute-done((bf16[512,256]{1,0:T(8,128)(2,1)}, bf16[512,256]{1,0:T(8,128)(2,1)S(1)}, u32[]{:S(2)}, u32[]{:S(2)}) %collective-permute-start.11) | collective-permute-done | bytes 262176 | tf_op jit(solution)/shard_map/ppermute | solution.py:37
  34.5 4.6 %project_sums.2 = (f32[3,512,256]{2,1,0:T(8,128)S(1)}, f32[512,1]{1,0:T(8,128)S(1)}) custom-call(s32[8]{0:T(128)S(1)} %gather_fusion.1, bf16[512,256]{1,0:T(8,128)(2,1)S(1)} %copy-done.5, bf16[512,256]{1,0:T(8,128)(2,1)S(1)} %collective-permute-done.9.refs_1_, bf16[512,256]{1,0:T(8,128)(2,1)S(1)} %collective-permute-done.2.refs_2_, ...), custom_call_target="tpu_custom_call" | custom-call | flops 1610612736 | bytes 8912896 | tf_op jit(solution)/shard_map/project_sums/pallas_call | solution.py:179
  40.7 2.8 %project_product.1.extended = bf16[512,256]{1,0:T(8,128)(2,1)S(1)} custom-call(s32[8]{0:T(128)S(1)} %gather_fusion, bf16[512,256]{1,0:T(8,128)(2,1)S(1)} %collective-permute-done.refs_0_, bf16[512,256]{1,0:T(8,128)(2,1)S(1)} %collective-permute-done.1.refs_1_, bf16[512,256]{1,0:T(8,128)(2,1)S(1)} %collective-permute-done.3.refs_2_, ...), custom_call_target="tpu_custom_call" | custom-call | flops 1073741824 | bytes 6815744 | tf_op jit(solution)/shard_map/project_product/pallas_call | solution.py:179
  44.9 7.3 %filtered.3 = bf16[384,256]{1,0:T(8,128)(2,1)S(1)} custom-call(bf16[512,256]{1,0:T(8,128)(2,1)S(1)} %project_product.1.extended, f32[128,256]{1,0:T(8,128)S(1)} %copy-done.27, s32[384,1]{1,0:T(8,128)S(1)} %copy-done.20, bf16[384,256]{1,0:T(8,128)(2,1)S(1)} %slice.222.gate), custom_call_target="tpu_custom_call" | custom-call | flops 3019898880 | bytes 786432 | tf_op jit(solution)/shard_map/filtered/pallas_call | solution.py:263
  63.6 3.2 %collective-permute-start.18 = (bf16[2,512,256]{2,1,0:T(8,128)(2,1)S(1)}, bf16[2,512,256]{2,1,0:T(8,128)(2,1)S(1)}, u32[]{:S(2)}, u32[]{:S(2)}) collective-permute-start(bf16[2,512,256]{2,1,0:T(8,128)(2,1)S(1)} %pad_maximum_fusion.1), channel_id=1, source_target_pairs={{0,6},{1,7},{2,0},{3,1},{4,2},{5,3},{6,4},{7,5},{8,14},{9,15},{10,... | collective-permute-start | bytes 1572872 | tf_op jit(solution)/shard_map/ppermute | solution.py:37
  67.1 11.4 %collective-permute-done.18 = bf16[2,512,256]{2,1,0:T(8,128)(2,1)S(1)} collective-permute-done((bf16[2,512,256]{2,1,0:T(8,128)(2,1)S(1)}, bf16[2,512,256]{2,1,0:T(8,128)(2,1)S(1)}, u32[]{:S(2)}, u32[]{:S(2)}) %collective-permute-start.18) | collective-permute-done | bytes 524320 | tf_op jit(solution)/shard_map/ppermute | solution.py:37
  78.4 3.7 %collective-permute-done.17 = bf16[2,512,256]{2,1,0:T(8,128)(2,1)S(1)} collective-permute-done((bf16[2,512,256]{2,1,0:T(8,128)(2,1)S(1)}, bf16[2,512,256]{2,1,0:T(8,128)(2,1)S(1)}, u32[]{:S(2)}, u32[]{:S(2)}) %collective-permute-start.17) | collective-permute-done | bytes 524320 | tf_op jit(solution)/shard_map/ppermute | solution.py:37
  85.5 7.2 %collective-permute-done.19 = bf16[512,256]{1,0:T(8,128)(2,1)S(1)} collective-permute-done((bf16[512,256]{1,0:T(8,128)(2,1)S(1)}, bf16[512,256]{1,0:T(8,128)(2,1)S(1)}, u32[]{:S(2)}, u32[]{:S(2)}) %collective-permute-start.19) | collective-permute-done | bytes 262176 | tf_op jit(solution)/shard_map/ppermute | solution.py:37
  96.6 5.2 %collective-permute-done.20 = bf16[512,256]{1,0:T(8,128)(2,1)S(1)} collective-permute-done((bf16[512,256]{1,0:T(8,128)(2,1)S(1)}, bf16[512,256]{1,0:T(8,128)(2,1)S(1)}, u32[]{:S(2)}, u32[]{:S(2)}) %collective-permute-start.20) | collective-permute-done | bytes 262176 | tf_op jit(solution)/shard_map/ppermute | solution.py:37
  106.6 3.6 %collective-permute-done.24.refs_2_ = bf16[512,256]{1,0:T(8,128)(2,1)S(1)} collective-permute-done((bf16[512,256]{1,0:T(8,128)(2,1)S(1)}, bf16[512,256]{1,0:T(8,128)(2,1)S(1)}, u32[]{:S(2)}, u32[]{:S(2)}) %collective-permute-start.24) | collective-permute-done | bytes 262176 | tf_op jit(solution)/shard_map/ppermute | solution.py:37
  110.2 3.7 %collective-permute-done.22.refs_0_ = bf16[512,256]{1,0:T(8,128)(2,1)S(1)} collective-permute-done((bf16[512,256]{1,0:T(8,128)(2,1)S(1)}, bf16[512,256]{1,0:T(8,128)(2,1)S(1)}, u32[]{:S(2)}, u32[]{:S(2)}) %collective-permute-start.22) | collective-permute-done | bytes 262176 | tf_op jit(solution)/shard_map/ppermute | solution.py:37
  113.9 3.5 %collective-permute-done.33.refs_4_ = bf16[512,256]{1,0:T(8,128)(2,1)S(1)} collective-permute-done((bf16[512,256]{1,0:T(8,128)(2,1)S(1)}, bf16[512,256]{1,0:T(8,128)(2,1)S(1)}, u32[]{:S(2)}, u32[]{:S(2)}) %collective-permute-start.33) | collective-permute-done | bytes 262176 | tf_op jit(solution)/shard_map/ppermute | solution.py:37
  124.9 3.4 %project_sums.3 = (f32[3,512,256]{2,1,0:T(8,128)S(1)}, f32[512,1]{1,0:T(8,128)S(1)}) custom-call(s32[8]{0:T(128)S(1)} %gather_fusion.1, bf16[512,256]{1,0:T(8,128)(2,1)S(1)} %get-tuple-element.19.refs_0_, bf16[512,256]{1,0:T(8,128)(2,1)S(1)} %collective-permute-done.31.refs_1_, bf16[512,256]{1,0:T(8,128)(2,1)S(1)} %collective-permute-done.24.refs_2_, ...), custom_call_target="tpu_custom_call" | custom-call | flops 1610612736 | bytes 8912896 | tf_op jit(solution)/shard_map/project_sums/pallas_call | solution.py:179
  128.4 2.9 %project_keys.1.refs_0_ = bf16[512,512]{1,0:T(8,128)(2,1)S(1)} custom-call(s32[8]{0:T(128)S(1)} %gather_fusion, bf16[512,256]{1,0:T(8,128)(2,1)S(1)} %collective-permute-done.22.refs_0_, bf16[512,256]{1,0:T(8,128)(2,1)S(1)} %collective-permute-done.23.refs_1_, bf16[512,256]{1,0:T(8,128)(2,1)S(1)} %collective-permute-done.25.refs_2_, ...), custom_call_target="tpu_custom_call" | custom-call | flops 1073741824 | bytes 6815744 | tf_op jit(solution)/shard_map/project_keys/pallas_call | solution.py:179
  136.1 12.7 %collective-permute-done.37.refs_0_ = bf16[512,512]{1,0:T(8,128)(2,1)} collective-permute-done((bf16[512,512]{1,0:T(8,128)(2,1)S(1)}, bf16[512,512]{1,0:T(8,128)(2,1)}, u32[]{:S(2)}, u32[]{:S(2)}) %collective-permute-start.37) | collective-permute-done | bytes 524320 | tf_op jit(solution)/shard_map/ppermute | solution.py:37
  148.8 4.3 %collective-permute-start.39 = (bf16[512,512]{1,0:T(8,128)(2,1)}, bf16[512,512]{1,0:T(8,128)(2,1)}, u32[]{:S(2)}, u32[]{:S(2)}) collective-permute-start(bf16[512,512]{1,0:T(8,128)(2,1)} %collective-permute-done.37.refs_0_), channel_id=1, source_target_pairs={{64,112},{80,64},{96,80},{112,96},{65,113},{81,65},{97,81},{113,97... | collective-permute-start | bytes 1572872 | tf_op jit(solution)/shard_map/ppermute | solution.py:37
  156.7 3.1 %collective-permute-start.45 = (bf16[256,512]{1,0:T(8,128)(2,1)}, bf16[256,512]{1,0:T(8,128)(2,1)}, u32[]{:S(2)}, u32[]{:S(2)}) collective-permute-start(bf16[256,512]{1,0:T(8,128)(2,1)} %slice.246), channel_id=1, source_target_pairs={{48,32},{0,48},{112,96},{64,112},{49,33},{1,49},{113,97},{65,113},... | collective-permute-start | bytes 786440 | tf_op jit(solution)/shard_map/ppermute | solution.py:37
  162.8 2.8 %copy-done.2 = bf16[4096,3,256]{2,0,1:T(8,128)(2,1)S(1)} copy-done((bf16[4096,3,256]{2,0,1:T(8,128)(2,1)S(1)}, bf16[4096,3,256]{2,0,1:T(8,128)(2,1)}, u32[]{:S(2)}) %copy-start.2) | copy-done | bytes 6291480
  171.1 2.8 %collective-permute-done.44 = bf16[256,512]{1,0:T(8,128)(2,1)} collective-permute-done((bf16[256,512]{1,0:T(8,128)(2,1)}, bf16[256,512]{1,0:T(8,128)(2,1)}, u32[]{:S(2)}, u32[]{:S(2)}) %collective-permute-start.44) | collective-permute-done | bytes 262176 | tf_op jit(solution)/shard_map/ppermute | solution.py:37
  176.0 2.8 %collective-permute-start.41 = (bf16[256,512]{1,0:T(8,128)(2,1)S(1)}, bf16[256,512]{1,0:T(8,128)(2,1)S(1)}, u32[]{:S(2)}, u32[]{:S(2)}) collective-permute-start(bf16[256,512]{1,0:T(8,128)(2,1)S(1)} %slice.244), channel_id=1, source_target_pairs={{112,96},{64,112},{80,64},{96,80},{113,97},{65,113},{81,65},{97,81... | collective-permute-start | bytes 786440 | tf_op jit(solution)/shard_map/ppermute | solution.py:37
  179.7 4.5 %collective-permute-start.40 = (bf16[256,512]{1,0:T(8,128)(2,1)S(1)}, bf16[256,512]{1,0:T(8,128)(2,1)S(1)}, u32[]{:S(2)}, u32[]{:S(2)}) collective-permute-start(bf16[256,512]{1,0:T(8,128)(2,1)S(1)} %slice.243), channel_id=1, source_target_pairs={{80,96},{96,112},{112,64},{64,80},{81,97},{97,113},{113,65},{65,81... | collective-permute-start | bytes 786440 | tf_op jit(solution)/shard_map/ppermute | solution.py:37
  184.3 13.1 %attend_near.1 = (f32[2,512,1]{2,1,0:T(8,128)S(1)}, f32[2,512,1]{2,1,0:T(8,128)S(1)}, f32[2,512,128]{2,1,0:T(8,128)S(1)}) custom-call(s32[1]{0:T(128)} %bitcast.25.me_ref, bf16[512,256]{1,0:T(8,128)(2,1)S(1)} %project_rotate.1.q_ref, s32[512,1]{1,0:T(8,128)S(1)} %copy-done.19, bf16[512,512]{1,0:T(8,128)(2,1)S(1)} %copy-done.16, ...), custom_call_target="tpu_custom_call" | custom-call | flops 3221225472 | bytes 2621440 | tf_op jit(solution)/shard_map/attend_near/pallas_call | solution.py:363
  197.4 14.8 %attend_far.1.x = bf16[512,256]{1,0:T(8,128)(2,1)S(1)} custom-call(s32[1]{0:T(128)} %bitcast.25.me_ref, bf16[512,256]{1,0:T(8,128)(2,1)S(1)} %project_rotate.1.q_ref, s32[512,1]{1,0:T(8,128)S(1)} %copy-done.19, bf16[512,512]{1,0:T(8,128)(2,1)} %collective-permute-done.37.refs_0_, bf16[512,512]{1,0:T(8,128)(2,1)} %collective-permute-done.38.refs_1_, ...), custom_call_target="tpu_custom_call" | custom-call | flops 3221225472 | bytes 2621440 | tf_op jit(solution)/shard_map/attend_far/pallas_call | solution.py:363
  214.9 2.9 %collective-permute-done.46 = bf16[8,512,256]{2,1,0:T(8,128)(2,1)S(1)} collective-permute-done((bf16[8,512,256]{2,1,0:T(8,128)(2,1)S(1)}, bf16[8,512,256]{2,1,0:T(8,128)(2,1)S(1)}, u32[]{:S(2)}, u32[]{:S(2)}) %collective-permute-start.46) | collective-permute-done | bytes 2097184 | tf_op jit(solution)/shard_map/ppermute | solution.py:37
  218.1 2.8 %collective-permute-start.48 = (bf16[2,512,256]{2,1,0:T(8,128)(2,1)S(1)}, bf16[2,512,256]{2,1,0:T(8,128)(2,1)S(1)}, u32[]{:S(2)}, u32[]{:S(2)}) collective-permute-start(bf16[2,512,256]{2,1,0:T(8,128)(2,1)S(1)} %pad_maximum_fusion.5), channel_id=1, source_target_pairs={{0,6},{1,7},{2,0},{3,1},{4,2},{5,3},{6,4},{7,5},{8,14},{9,15},{10,... | collective-permute-start | bytes 1572872 | tf_op jit(solution)/shard_map/ppermute | solution.py:37
  221.0 11.3 %collective-permute-done.48 = bf16[2,512,256]{2,1,0:T(8,128)(2,1)S(1)} collective-permute-done((bf16[2,512,256]{2,1,0:T(8,128)(2,1)S(1)}, bf16[2,512,256]{2,1,0:T(8,128)(2,1)S(1)}, u32[]{:S(2)}, u32[]{:S(2)}) %collective-permute-start.48) | collective-permute-done | bytes 524320 | tf_op jit(solution)/shard_map/ppermute | solution.py:37
  232.4 3.5 %collective-permute-done.47 = bf16[2,512,256]{2,1,0:T(8,128)(2,1)S(1)} collective-permute-done((bf16[2,512,256]{2,1,0:T(8,128)(2,1)S(1)}, bf16[2,512,256]{2,1,0:T(8,128)(2,1)S(1)}, u32[]{:S(2)}, u32[]{:S(2)}) %collective-permute-start.47) | collective-permute-done | bytes 524320 | tf_op jit(solution)/shard_map/ppermute | solution.py:37
  238.2 7.2 %collective-permute-done.49 = bf16[512,256]{1,0:T(8,128)(2,1)S(1)} collective-permute-done((bf16[512,256]{1,0:T(8,128)(2,1)S(1)}, bf16[512,256]{1,0:T(8,128)(2,1)S(1)}, u32[]{:S(2)}, u32[]{:S(2)}) %collective-permute-start.49) | collective-permute-done | bytes 262176 | tf_op jit(solution)/shard_map/ppermute | solution.py:37
  245.6 3.4 %collective-permute-done.51 = bf16[512,256]{1,0:T(8,128)(2,1)S(1)} collective-permute-done((bf16[512,256]{1,0:T(8,128)(2,1)S(1)}, bf16[512,256]{1,0:T(8,128)(2,1)S(1)}, u32[]{:S(2)}, u32[]{:S(2)}) %collective-permute-start.51) | collective-permute-done | bytes 262176 | tf_op jit(solution)/shard_map/ppermute | solution.py:37
  249.0 4.5 %collective-permute-done.50 = bf16[512,256]{1,0:T(8,128)(2,1)S(1)} collective-permute-done((bf16[512,256]{1,0:T(8,128)(2,1)S(1)}, bf16[512,256]{1,0:T(8,128)(2,1)S(1)}, u32[]{:S(2)}, u32[]{:S(2)}) %collective-permute-start.50) | collective-permute-done | bytes 262176 | tf_op jit(solution)/shard_map/ppermute | solution.py:37
  (191 shorter events, 81.6 us)
Async XLA Ops:
  1.3 11.3 %collective-permute-start = (bf16[512,256]{1,0:T(8,128)(2,1)}, bf16[512,256]{1,0:T(8,128)(2,1)S(1)}, u32[]{:S(2)}, u32[]{:S(2)}) collective-permute-start(bf16[512,256]{1,0:T(8,128)(2,1)} %refs_0_.1), channel_id=1, source_target_pairs={{0,4},{1,5},{2,6},{3,7},{4,0},{5,1},{6,2},{7,3},{8,12},{9,13},{10,... | collective-permute-start | bytes 786440 | tf_op jit(solution)/shard_map/ppermute | solution.py:37
  5.2 14.1 %collective-permute-start.11 = (bf16[512,256]{1,0:T(8,128)(2,1)}, bf16[512,256]{1,0:T(8,128)(2,1)S(1)}, u32[]{:S(2)}, u32[]{:S(2)}) collective-permute-start(bf16[512,256]{1,0:T(8,128)(2,1)} %refs_0_.1), channel_id=1, source_target_pairs={{0,6},{1,7},{2,0},{3,1},{4,2},{5,3},{6,4},{7,5},{8,14},{9,15},{10,... | collective-permute-start | bytes 786440 | tf_op jit(solution)/shard_map/ppermute | solution.py:37
  5.9 14.1 %collective-permute-start.13 = (bf16[512,256]{1,0:T(8,128)(2,1)}, bf16[512,256]{1,0:T(8,128)(2,1)S(1)}, u32[]{:S(2)}, u32[]{:S(2)}) collective-permute-start(bf16[512,256]{1,0:T(8,128)(2,1)} %refs_0_.1), channel_id=1, source_target_pairs={{0,2},{1,3},{2,4},{3,5},{4,6},{5,7},{6,0},{7,1},{8,10},{9,11},{10,... | collective-permute-start | bytes 786440 | tf_op jit(solution)/shard_map/ppermute | solution.py:37
  8.3 15.2 %collective-permute-start.3 = (bf16[512,256]{1,0:T(8,128)(2,1)S(1)}, bf16[512,256]{1,0:T(8,128)(2,1)S(1)}, u32[]{:S(2)}, u32[]{:S(2)}) collective-permute-start(bf16[512,256]{1,0:T(8,128)(2,1)S(1)} %collective-permute-done.2.refs_2_), channel_id=1, source_target_pairs={{0,6},{1,7},{2,0},{3,1},{4,2},{5,3},{6,4},{7,5},{8,14},{9,15},{10,... | collective-permute-start | bytes 786440 | tf_op jit(solution)/shard_map/ppermute | solution.py:37
  12.6 10.8 %collective-permute-start.5 = (bf16[512,256]{1,0:T(8,128)(2,1)S(1)}, bf16[512,256]{1,0:T(8,128)(2,1)S(1)}, u32[]{:S(2)}, u32[]{:S(2)}) collective-permute-start(bf16[512,256]{1,0:T(8,128)(2,1)S(1)} %collective-permute-done.2.refs_2_), channel_id=1, source_target_pairs={{0,2},{1,3},{2,4},{3,5},{4,6},{5,7},{6,0},{7,1},{8,10},{9,11},{10,... | collective-permute-start | bytes 786440 | tf_op jit(solution)/shard_map/ppermute | solution.py:37
  14.2 11.5 %collective-permute-start.10 = (bf16[512,256]{1,0:T(8,128)(2,1)S(1)}, bf16[512,256]{1,0:T(8,128)(2,1)S(1)}, u32[]{:S(2)}, u32[]{:S(2)}) collective-permute-start(bf16[512,256]{1,0:T(8,128)(2,1)S(1)} %collective-permute-done.2.refs_2_), channel_id=1, source_target_pairs={{0,1},{1,0},{2,3},{3,2},{4,5},{5,4},{6,7},{7,6},{8,9},{9,8},{10,11... | collective-permute-start | bytes 786440 | tf_op jit(solution)/shard_map/ppermute | solution.py:37
  23.4 15.7 %collective-permute-start.1 = (bf16[512,256]{1,0:T(8,128)(2,1)S(1)}, bf16[512,256]{1,0:T(8,128)(2,1)S(1)}, u32[]{:S(2)}, u32[]{:S(2)}) collective-permute-start(bf16[512,256]{1,0:T(8,128)(2,1)S(1)} %collective-permute-done.refs_0_), channel_id=1, source_target_pairs={{0,1},{1,0},{2,3},{3,2},{4,5},{5,4},{6,7},{7,6},{8,9},{9,8},{10,11... | collective-permute-start | bytes 786440 | tf_op jit(solution)/shard_map/ppermute | solution.py:37
  25.6 13.5 %collective-permute-start.4 = (bf16[512,256]{1,0:T(8,128)(2,1)S(1)}, bf16[512,256]{1,0:T(8,128)(2,1)S(1)}, u32[]{:S(2)}, u32[]{:S(2)}) collective-permute-start(bf16[512,256]{1,0:T(8,128)(2,1)S(1)} %collective-permute-done.3.refs_2_), channel_id=1, source_target_pairs={{0,1},{1,0},{2,3},{3,2},{4,5},{5,4},{6,7},{7,6},{8,9},{9,8},{10,11... | collective-permute-start | bytes 786440 | tf_op jit(solution)/shard_map/ppermute | solution.py:37
  25.6 13.5 %collective-permute-start.6 = (bf16[512,256]{1,0:T(8,128)(2,1)S(1)}, bf16[512,256]{1,0:T(8,128)(2,1)S(1)}, u32[]{:S(2)}, u32[]{:S(2)}) collective-permute-start(bf16[512,256]{1,0:T(8,128)(2,1)S(1)} %collective-permute-done.5.refs_4_), channel_id=1, source_target_pairs={{0,1},{1,0},{2,3},{3,2},{4,5},{5,4},{6,7},{7,6},{8,9},{9,8},{10,11... | collective-permute-start | bytes 786440 | tf_op jit(solution)/shard_map/ppermute | solution.py:37
  26.8 12.3 %collective-permute-start.8 = (bf16[512,256]{1,0:T(8,128)(2,1)S(1)}, bf16[512,256]{1,0:T(8,128)(2,1)S(1)}, u32[]{:S(2)}, u32[]{:S(2)}) collective-permute-start(bf16[512,256]{1,0:T(8,128)(2,1)S(1)} %collective-permute-done.7.refs_6_), channel_id=1, source_target_pairs={{0,1},{1,0},{2,3},{3,2},{4,5},{5,4},{6,7},{7,6},{8,9},{9,8},{10,11... | collective-permute-start | bytes 786440 | tf_op jit(solution)/shard_map/ppermute | solution.py:37
  63.6 14.9 %collective-permute-start.18 = (bf16[2,512,256]{2,1,0:T(8,128)(2,1)S(1)}, bf16[2,512,256]{2,1,0:T(8,128)(2,1)S(1)}, u32[]{:S(2)}, u32[]{:S(2)}) collective-permute-start(bf16[2,512,256]{2,1,0:T(8,128)(2,1)S(1)} %pad_maximum_fusion.1), channel_id=1, source_target_pairs={{0,6},{1,7},{2,0},{3,1},{4,2},{5,3},{6,4},{7,5},{8,14},{9,15},{10,... | collective-permute-start | bytes 1572872 | tf_op jit(solution)/shard_map/ppermute | solution.py:37
  66.8 15.4 %collective-permute-start.17 = (bf16[2,512,256]{2,1,0:T(8,128)(2,1)S(1)}, bf16[2,512,256]{2,1,0:T(8,128)(2,1)S(1)}, u32[]{:S(2)}, u32[]{:S(2)}) collective-permute-start(bf16[2,512,256]{2,1,0:T(8,128)(2,1)S(1)} %pad_maximum_fusion), channel_id=1, source_target_pairs={{0,2},{1,3},{2,4},{3,5},{4,6},{5,7},{6,0},{7,1},{8,10},{9,11},{10,... | collective-permute-start | bytes 1572872 | tf_op jit(solution)/shard_map/ppermute | solution.py:37
  84.3 12.3 %collective-permute-start.21 = (bf16[512,256]{1,0:T(8,128)(2,1)S(1)}, bf16[512,256]{1,0:T(8,128)(2,1)S(1)}, u32[]{:S(2)}, u32[]{:S(2)}) collective-permute-start(bf16[512,256]{1,0:T(8,128)(2,1)S(1)} %get-tuple-element.28), channel_id=1, source_target_pairs={{0,8},{1,9},{2,10},{3,11},{4,12},{5,13},{6,14},{7,15},{8,0},{9,1},... | collective-permute-start | bytes 786440 | tf_op jit(solution)/shard_map/ppermute | solution.py:37
  104.5 9.4 %collective-permute-start.22 = (bf16[512,256]{1,0:T(8,128)(2,1)S(1)}, bf16[512,256]{1,0:T(8,128)(2,1)S(1)}, u32[]{:S(2)}, u32[]{:S(2)}) collective-permute-start(bf16[512,256]{1,0:T(8,128)(2,1)S(1)} %get-tuple-element.19.refs_0_), channel_id=1, source_target_pairs={{0,4},{1,5},{2,6},{3,7},{4,0},{5,1},{6,2},{7,3},{8,12},{9,13},{10,... | collective-permute-start | bytes 786440 | tf_op jit(solution)/shard_map/ppermute | solution.py:37
  104.5 9.4 %collective-permute-start.31 = (bf16[512,256]{1,0:T(8,128)(2,1)S(1)}, bf16[512,256]{1,0:T(8,128)(2,1)S(1)}, u32[]{:S(2)}, u32[]{:S(2)}) collective-permute-start(bf16[512,256]{1,0:T(8,128)(2,1)S(1)} %get-tuple-element.19.refs_0_), channel_id=1, source_target_pairs={{0,1},{1,0},{2,3},{3,2},{4,5},{5,4},{6,7},{7,6},{8,9},{9,8},{10,11... | collective-permute-start | bytes 786440 | tf_op jit(solution)/shard_map/ppermute | solution.py:37
  104.5 12.9 %collective-permute-start.33 = (bf16[512,256]{1,0:T(8,128)(2,1)S(1)}, bf16[512,256]{1,0:T(8,128)(2,1)S(1)}, u32[]{:S(2)}, u32[]{:S(2)}) collective-permute-start(bf16[512,256]{1,0:T(8,128)(2,1)S(1)} %get-tuple-element.19.refs_0_), channel_id=1, source_target_pairs={{0,6},{1,7},{2,0},{3,1},{4,2},{5,3},{6,4},{7,5},{8,14},{9,15},{10,... | collective-permute-start | bytes 786440 | tf_op jit(solution)/shard_map/ppermute | solution.py:37
  106.3 12.4 %collective-permute-start.35 = (bf16[512,256]{1,0:T(8,128)(2,1)S(1)}, bf16[512,256]{1,0:T(8,128)(2,1)S(1)}, u32[]{:S(2)}, u32[]{:S(2)}) collective-permute-start(bf16[512,256]{1,0:T(8,128)(2,1)S(1)} %get-tuple-element.19.refs_0_), channel_id=1, source_target_pairs={{0,2},{1,3},{2,4},{3,5},{4,6},{5,7},{6,0},{7,1},{8,10},{9,11},{10,... | collective-permute-start | bytes 786440 | tf_op jit(solution)/shard_map/ppermute | solution.py:37
  110.1 10.8 %collective-permute-start.25 = (bf16[512,256]{1,0:T(8,128)(2,1)S(1)}, bf16[512,256]{1,0:T(8,128)(2,1)S(1)}, u32[]{:S(2)}, u32[]{:S(2)}) collective-permute-start(bf16[512,256]{1,0:T(8,128)(2,1)S(1)} %collective-permute-done.24.refs_2_), channel_id=1, source_target_pairs={{0,6},{1,7},{2,0},{3,1},{4,2},{5,3},{6,4},{7,5},{8,14},{9,15},{10,... | collective-permute-start | bytes 786440 | tf_op jit(solution)/shard_map/ppermute | solution.py:37
  113.9 9.8 %collective-permute-start.27 = (bf16[512,256]{1,0:T(8,128)(2,1)S(1)}, bf16[512,256]{1,0:T(8,128)(2,1)S(1)}, u32[]{:S(2)}, u32[]{:S(2)}) collective-permute-start(bf16[512,256]{1,0:T(8,128)(2,1)S(1)} %collective-permute-done.24.refs_2_), channel_id=1, source_target_pairs={{0,2},{1,3},{2,4},{3,5},{4,6},{5,7},{6,0},{7,1},{8,10},{9,11},{10,... | collective-permute-start | bytes 786440 | tf_op jit(solution)/shard_map/ppermute | solution.py:37
  113.9 10.3 %collective-permute-start.32 = (bf16[512,256]{1,0:T(8,128)(2,1)S(1)}, bf16[512,256]{1,0:T(8,128)(2,1)S(1)}, u32[]{:S(2)}, u32[]{:S(2)}) collective-permute-start(bf16[512,256]{1,0:T(8,128)(2,1)S(1)} %collective-permute-done.24.refs_2_), channel_id=1, source_target_pairs={{0,1},{1,0},{2,3},{3,2},{4,5},{5,4},{6,7},{7,6},{8,9},{9,8},{10,11... | collective-permute-start | bytes 786440 | tf_op jit(solution)/shard_map/ppermute | solution.py:37
  131.4 17.4 %collective-permute-start.37 = (bf16[512,512]{1,0:T(8,128)(2,1)S(1)}, bf16[512,512]{1,0:T(8,128)(2,1)}, u32[]{:S(2)}, u32[]{:S(2)}) collective-permute-start(bf16[512,512]{1,0:T(8,128)(2,1)S(1)} %project_keys.1.refs_0_), channel_id=1, source_target_pairs={{0,64},{16,80},{32,96},{48,112},{1,65},{17,81},{33,97},{49,113},{2... | collective-permute-start | bytes 1572872 | tf_op jit(solution)/shard_map/ppermute | solution.py:37
  132.7 23.2 %collective-permute-start.43 = (bf16[512,512]{1,0:T(8,128)(2,1)S(1)}, bf16[512,512]{1,0:T(8,128)(2,1)S(1)}, u32[]{:S(2)}, u32[]{:S(2)}) collective-permute-start(bf16[512,512]{1,0:T(8,128)(2,1)S(1)} %project_keys.1.refs_0_), channel_id=1, source_target_pairs={{0,48},{16,0},{64,112},{80,64},{1,49},{17,1},{65,113},{81,65},{2,5... | collective-permute-start | bytes 1572872 | tf_op jit(solution)/shard_map/ppermute | solution.py:37
  134.0 25.8 %collective-permute-start.42 = (bf16[512,512]{1,0:T(8,128)(2,1)S(1)}, bf16[512,512]{1,0:T(8,128)(2,1)S(1)}, u32[]{:S(2)}, u32[]{:S(2)}) collective-permute-start(bf16[512,512]{1,0:T(8,128)(2,1)S(1)} %project_keys.1.refs_0_), channel_id=1, source_target_pairs={{0,16},{16,32},{32,48},{64,80},{80,96},{96,112},{1,17},{17,33},{33... | collective-permute-start | bytes 1572872 | tf_op jit(solution)/shard_map/ppermute | solution.py:37
  148.8 26.2 %collective-permute-start.39 = (bf16[512,512]{1,0:T(8,128)(2,1)}, bf16[512,512]{1,0:T(8,128)(2,1)}, u32[]{:S(2)}, u32[]{:S(2)}) collective-permute-start(bf16[512,512]{1,0:T(8,128)(2,1)} %collective-permute-done.37.refs_0_), channel_id=1, source_target_pairs={{64,112},{80,64},{96,80},{112,96},{65,113},{81,65},{97,81},{113,97... | collective-permute-start | bytes 1572872 | tf_op jit(solution)/shard_map/ppermute | solution.py:37
  153.2 25.6 %collective-permute-start.38 = (bf16[512,512]{1,0:T(8,128)(2,1)}, bf16[512,512]{1,0:T(8,128)(2,1)}, u32[]{:S(2)}, u32[]{:S(2)}) collective-permute-start(bf16[512,512]{1,0:T(8,128)(2,1)} %collective-permute-done.37.refs_0_), channel_id=1, source_target_pairs={{64,80},{80,96},{96,112},{112,64},{65,81},{81,97},{97,113},{113,65... | collective-permute-start | bytes 1572872 | tf_op jit(solution)/shard_map/ppermute | solution.py:37
  156.7 14.4 %collective-permute-start.45 = (bf16[256,512]{1,0:T(8,128)(2,1)}, bf16[256,512]{1,0:T(8,128)(2,1)}, u32[]{:S(2)}, u32[]{:S(2)}) collective-permute-start(bf16[256,512]{1,0:T(8,128)(2,1)} %slice.246), channel_id=1, source_target_pairs={{48,32},{0,48},{112,96},{64,112},{49,33},{1,49},{113,97},{65,113},... | collective-permute-start | bytes 786440 | tf_op jit(solution)/shard_map/ppermute | solution.py:37
  160.7 13.2 %collective-permute-start.44 = (bf16[256,512]{1,0:T(8,128)(2,1)}, bf16[256,512]{1,0:T(8,128)(2,1)}, u32[]{:S(2)}, u32[]{:S(2)}) collective-permute-start(bf16[256,512]{1,0:T(8,128)(2,1)} %slice.245), channel_id=1, source_target_pairs={{16,32},{32,48},{80,96},{96,112},{17,33},{33,49},{81,97},{97,113},... | collective-permute-start | bytes 786440 | tf_op jit(solution)/shard_map/ppermute | solution.py:37
  176.0 21.4 %collective-permute-start.41 = (bf16[256,512]{1,0:T(8,128)(2,1)S(1)}, bf16[256,512]{1,0:T(8,128)(2,1)S(1)}, u32[]{:S(2)}, u32[]{:S(2)}) collective-permute-start(bf16[256,512]{1,0:T(8,128)(2,1)S(1)} %slice.244), channel_id=1, source_target_pairs={{112,96},{64,112},{80,64},{96,80},{113,97},{65,113},{81,65},{97,81... | collective-permute-start | bytes 786440 | tf_op jit(solution)/shard_map/ppermute | solution.py:37
  179.7 17.6 %collective-permute-start.40 = (bf16[256,512]{1,0:T(8,128)(2,1)S(1)}, bf16[256,512]{1,0:T(8,128)(2,1)S(1)}, u32[]{:S(2)}, u32[]{:S(2)}) collective-permute-start(bf16[256,512]{1,0:T(8,128)(2,1)S(1)} %slice.243), channel_id=1, source_target_pairs={{80,96},{96,112},{112,64},{64,80},{81,97},{97,113},{113,65},{65,81... | collective-permute-start | bytes 786440 | tf_op jit(solution)/shard_map/ppermute | solution.py:37
  218.1 14.3 %collective-permute-start.48 = (bf16[2,512,256]{2,1,0:T(8,128)(2,1)S(1)}, bf16[2,512,256]{2,1,0:T(8,128)(2,1)S(1)}, u32[]{:S(2)}, u32[]{:S(2)}) collective-permute-start(bf16[2,512,256]{2,1,0:T(8,128)(2,1)S(1)} %pad_maximum_fusion.5), channel_id=1, source_target_pairs={{0,6},{1,7},{2,0},{3,1},{4,2},{5,3},{6,4},{7,5},{8,14},{9,15},{10,... | collective-permute-start | bytes 1572872 | tf_op jit(solution)/shard_map/ppermute | solution.py:37
  220.9 15.0 %collective-permute-start.47 = (bf16[2,512,256]{2,1,0:T(8,128)(2,1)S(1)}, bf16[2,512,256]{2,1,0:T(8,128)(2,1)S(1)}, u32[]{:S(2)}, u32[]{:S(2)}) collective-permute-start(bf16[2,512,256]{2,1,0:T(8,128)(2,1)S(1)} %pad_maximum_fusion.4), channel_id=1, source_target_pairs={{0,2},{1,3},{2,4},{3,5},{4,6},{5,7},{6,0},{7,1},{8,10},{9,11},{10,... | collective-permute-start | bytes 1572872 | tf_op jit(solution)/shard_map/ppermute | solution.py:37
  237.4 11.6 %collective-permute-start.51 = (bf16[512,256]{1,0:T(8,128)(2,1)S(1)}, bf16[512,256]{1,0:T(8,128)(2,1)S(1)}, u32[]{:S(2)}, u32[]{:S(2)}) collective-permute-start(bf16[512,256]{1,0:T(8,128)(2,1)S(1)} %get-tuple-element.22), channel_id=1, source_target_pairs={{0,8},{1,9},{2,10},{3,11},{4,12},{5,13},{6,14},{7,15},{8,0},{9,1},... | collective-permute-start | bytes 786440 | tf_op jit(solution)/shard_map/ppermute | solution.py:37
  (51 other events, 460.3 us)
